TPU v7x, 512 devices: a whole 4x4x16 slice. The times are simulated.
512 devices in a mesh: seq: 32 (over z, y_lo), mp: 16 (over x, y_hi, core).
Axes of the slice: x: 4, y: 4 (y_hi: 2, y_lo: 2; y = y_hi * 2 + y_lo), z: 16, core: 2. Of those that a mesh axis runs over, the one named last changes fastest.
Arguments:
- queries: bfloat16 [16384, 8192], P('seq', 'mp'), may hold values from -6 to 6
- keys_in: bfloat16 [16384, 8192], P('seq', 'mp'), may hold values from -6 to 6
- values_in: bfloat16 [16384, 8192], P('seq', 'mp'), may hold values from -6 to 6
- residual: bfloat16 [16384, 8192], P('seq', 'mp')
- short_taps: bfloat16 [3, 7, 8192], P(None, None, 'mp'), may hold values from -2 to 2
- mr_filter: bfloat16 [128, 512], P('seq', 'mp'), may hold values from -0.5 to 0.5
- norm_gain: bfloat16 [8192], P('mp'), may hold values from 0.5 to 1.5
- predecessor: int32 [32], replicated, may hold values from -1 to 31, as said below
- stretch_lengths: int32 [32], replicated, may hold values from 1 to 512, as said below
Outputs:
- mixed: bfloat16 [16384, 8192], P('seq', 'mp')
- normed: bfloat16 [16384, 8192], P('seq', 'mp')
Inputs may be any that keep to these rules, and one draw needn't show every extreme that they name: predecessor[j] is the stretch holding the preceding 512 tokens of stretch j's genome, or -1 for a genome's first stretch; each stretch precedes at most one stretch, and the chains have no cycles. `stretch_lengths`: every stretch that precedes another stretch is full (512 valid tokens); valid tokens come first.
All inputs are finite; a program needn't handle non-finite values.
Results may differ from a plain program's by a relative error of at most 0.0049.
Values may be sent and summed in bfloat16 or wider, within the bound.
A program may use at most 64 MiB of HBM per device.

v0:
```python
import jax
import jax.numpy as jnp
from jax import lax
from jax.sharding import PartitionSpec as P

EPSILON = 1e-06


def featurize(extended, taps):
    length = extended.shape[0] - 8
    total = jnp.zeros((length, extended.shape[1]), jnp.float32)
    for offset in range(taps.shape[0]):
        total = total + taps[offset].astype(jnp.float32) * extended[
            8 - offset : 8 - offset + length
        ].astype(jnp.float32)
    return total


def toeplitz_blocks(filter_rows):
    tap_count = filter_rows.shape[0]
    group_count = filter_rows.shape[1]
    flipped = filter_rows[::-1].T
    pattern = jnp.concatenate(
        [
            jnp.zeros((group_count, 1), filter_rows.dtype),
            flipped,
            jnp.zeros((group_count, tap_count), filter_rows.dtype),
        ],
        axis=1,
    )
    tiled = jnp.tile(pattern, (1, tap_count))[:, : 2 * tap_count * tap_count]
    return tiled.reshape(group_count, tap_count, 2 * tap_count)


def long_conv(extended, filter_rows, group_size):
    tap_count = filter_rows.shape[0]
    length = extended.shape[0] - tap_count
    blocks = length // tap_count
    channels = extended.shape[1]
    pieces = extended.reshape(blocks + 1, tap_count, channels)
    windows = jnp.concatenate([pieces[:-1], pieces[1:]], axis=1).reshape(
        blocks, 2 * tap_count, channels // group_size, group_size
    )
    matrices = toeplitz_blocks(filter_rows)
    result = jnp.einsum("gij,bjgc->bigc", matrices, windows, preferred_element_type=jnp.float32)
    return result.reshape(length, channels)


def body(
    queries,
    keys_in,
    values_in,
    residual,
    short_taps,
    mr_filter,
    norm_gain,
    predecessor,
    stretch_lengths,
):
    row_count, width = queries.shape
    device = lax.axis_index("seq")
    filter_rows = lax.all_gather(mr_filter, "seq", axis=0, tiled=True)
    tap_count = filter_rows.shape[0]
    group_size = width // filter_rows.shape[1]
    blank = jnp.zeros((8, width), queries.dtype)
    key_feat = featurize(jnp.concatenate([blank, keys_in]), short_taps[1])
    value_feat = featurize(jnp.concatenate([blank, values_in]), short_taps[2])
    mixed_in = (key_feat * value_feat).astype(jnp.bfloat16)
    state_tail = mixed_in[row_count - tap_count :][None]
    raw_tail = jnp.concatenate(
        [queries[row_count - 8 :], keys_in[row_count - 8 :], values_in[row_count - 8 :]], axis=1
    )[None]
    source = predecessor[device]
    carry = (jnp.zeros_like(state_tail), jnp.zeros_like(raw_tail))
    piece = (
        lax.all_gather(state_tail, "seq", axis=0, tiled=True),
        lax.all_gather(raw_tail, "seq", axis=0, tiled=True),
    )
    count = piece[0].shape[0]
    inside = (source >= 0) & (source < count)
    offset = jnp.clip(source, 0, count - 1)
    prev_state, prev_raw = tuple(
        (
            jnp.where(inside, lax.dynamic_slice_in_dim(member, offset, 1, 0), kept)
            for member, kept in zip(piece, carry)
        )
    )
    prev_rows = prev_raw[0]
    prev_query = prev_rows[:, :width]
    prev_key = prev_rows[:, width : 2 * width]
    prev_value = prev_rows[:, 2 * width :]
    query_feat = featurize(jnp.concatenate([prev_query, queries]), short_taps[0])
    head_key = featurize(jnp.concatenate([prev_key, keys_in[:8]]), short_taps[1])
    head_value = featurize(jnp.concatenate([prev_value, values_in[:8]]), short_taps[2])
    head_mixed = (head_key * head_value).astype(jnp.bfloat16)
    mixed_in = jnp.concatenate([head_mixed, mixed_in[8:]])
    extended = jnp.concatenate([prev_state[0], mixed_in])
    filtered = long_conv(extended, filter_rows, group_size)
    valid = (jnp.arange(row_count, dtype=jnp.int32) < stretch_lengths[device])[:, None]
    mixed = jnp.where(valid, query_feat * filtered, 0.0).astype(jnp.bfloat16)
    summed = residual.astype(jnp.float32) + mixed.astype(jnp.float32)
    squares_total = lax.psum(jnp.sum(summed * summed, axis=1), "mp")
    scale_rows = lax.rsqrt(squares_total / (width * lax.axis_size("mp")) + EPSILON)
    normed = jnp.where(
        valid, summed * scale_rows[:, None] * norm_gain.astype(jnp.float32), 0.0
    ).astype(jnp.bfloat16)
    return (mixed, normed)


def solution(mesh):
    in_specs = (
        P("seq", "mp"),
        P("seq", "mp"),
        P("seq", "mp"),
        P("seq", "mp"),
        P(None, None, "mp"),
        P("seq", "mp"),
        P("mp"),
        P(),
        P(),
    )
    out_specs = (P("seq", "mp"), P("seq", "mp"))
    return jax.shard_map(body, mesh=mesh, in_specs=in_specs, out_specs=out_specs, check_vma=False)
```

profile of v0, /device:TPU:1, one launch (start us, length us, event | category | flops | bytes accessed | tf_op | source)
XLA Modules:
  0.0 226.0 jit_solution(18346637916515088260)
XLA Ops:
  7.2 1.0 slice_convert_fusion.20
  8.2 0.8 slice_convert_fusion.1
  9.0 5.3 %multiply_convert_fusion = bf16[512,512]{1,0:T(8,128)(2,1)S(1)} fusion(bf16[512,512]{1,0:T(8,128)(2,1)} %param.11, bf16[512,512]{1,0:T(8,128)(2,1)} %param.10, f32[512]{0:T(512)S(1)} %bitcast.92, f32[512]{0:T(512)S(1)} %bitcast.90, f32[512]{0:T(512)S(1)} %bitcast.66, f32[512]{0:T(512)S(1)} %bitcast.68, f32[512]{0:T(512)S(1)} %bitcast.70, ...), kind=kLoop, calls=%fused_computation.17 | loop fusion | flops 11010048 | bytes 1601536 | tf_op jit(solution)/shard_map/convert_element_type | solution.py:68
  14.4 0.7 slice.328
  16.9 1.0 copy.66
  18.5 56.7 %all-gather.2 = bf16[32,4,32]{2,1,0:T(4,128)(2,1)S(1)} all-gather(bf16[1,4,32]{2,1,0:T(4,128)(2,1)S(1)} %bitcast.102), channel_id=1, replica_groups=mesh['seq'=32,'mp'=16] {'seq'}, dimensions={0}, use_global_device_ids=true | all-gather | bytes 8448 | tf_op jit(solution)/shard_map/all_gather | solution.py:62
  75.8 4.4 %tile.10 = bf16[32,32896]{1,0:T(8,128)(2,1)} reshape(bf16[32,128,257]{2,1,0:T(8,128)(2,1)S(1)} %tile.4) | data formatting | bytes 4210688 | tf_op jit(solution)/shard_map/tile | solution.py:31
  80.3 1.6 slice-done
  82.4 0.8 fusion.27
  83.2 59.5 %all-gather = bf16[256,1536]{1,0:T(8,128)(2,1)S(1)} all-gather(bf16[8,1536]{1,0:T(8,128)(2,1)S(1)} %pad_maximum_fusion.4), channel_id=2, replica_groups=mesh['seq'=32,'mp'=16] {'seq'}, dimensions={0}, use_global_device_ids=true | all-gather | bytes 811008 | tf_op jit(solution)/shard_map/all_gather | solution.py:77
  143.6 1.3 copy.75
  145.7 4.9 %all-gather.5.cloned.1.call-done = bf16[4096,512]{1,0:T(8,128)(2,1)} async-done(((bf16[128,512]{1,0:T(8,128)(2,1)}), bf16[4096,512]{1,0:T(8,128)(2,1)}) %all-gather.5.cloned.1.call-update) | async-done | bytes 4194320 | tf_op jit(solution)/shard_map/all_gather | solution.py:76
  150.6 0.9 select_bitcast_fusion
  151.5 1.0 pad_maximum_fusion
  152.6 2.1 copy.69
  154.7 2.0 concatenate.42
  156.7 1.9 copy.71
  158.6 1.0 copy.70
  159.6 1.2 concatenate.44
  160.9 1.9 fusion.2
  163.8 2.1 multiply_reduce_fusion
  165.9 51.0 %psum.7 = f32[512]{0:T(512)S(1)} all-reduce(f32[512]{0:T(512)S(1)} %get-tuple-element.8), channel_id=1, replica_groups=mesh['seq'=32,'mp'=16] {'mp'}, use_global_device_ids=true, to_apply=%region_1.2 | all-reduce | flops 512 | bytes 4096 | tf_op jit(solution)/shard_map/psum | solution.py:102
  216.9 1.0 copy.76
  218.1 1.0 copy.77
  (44 shorter events, 4.8 us)
Async XLA Ops:
  7.2 8.0 %copy-start.6 = (s32[32]{0:T(128)S(1)}, s32[32]{0:T(128)}, u32[]{:S(2)}) copy-start(s32[32]{0:T(128)} %param.16) | copy-start | bytes 388
  7.2 9.7 %copy-start.3 = (bf16[512,512]{1,0:T(8,128)(2,1)S(1)}, bf16[512,512]{1,0:T(8,128)(2,1)}, u32[]{:S(2)}) copy-start(bf16[512,512]{1,0:T(8,128)(2,1)} %param.9) | copy-start | bytes 1572868
  7.2 143.4 %all-gather.5.cloned.1.call-start = ((), (), s32[]{:S(2)}) async-start(), calls=%async_computation | async-start | bytes 4325376 | tf_op jit(solution)/shard_map/all_gather | solution.py:76
  8.2 10.2 %copy-start.4 = (bf16[4,32]{1,0:T(4,128)(2,1)S(1)}, bf16[4,32]{1,0:T(4,128)(2,1)}, u32[]{:S(2)}) copy-start(bf16[4,32]{1,0:T(4,128)(2,1)} %param.14) | copy-start | bytes 772
  14.4 61.1 %copy-start = (bf16[512,512]{1,0:T(8,128)(2,1)}, bf16[512,512]{1,0:T(8,128)(2,1)S(1)}, u32[]{:S(2)}) copy-start(bf16[512,512]{1,0:T(8,128)(2,1)S(1)} %multiply_convert_fusion) | copy-start | bytes 1572868
  80.3 1.6 slice-start
  81.9 1.3 slice-start.2
  81.9 61.1 %copy-start.7 = (s32[32]{0:T(128)S(1)}, s32[32]{0:T(128)}, u32[]{:S(2)}) copy-start(s32[32]{0:T(128)} %param.17) | copy-start | bytes 388
  82.4 62.5 %copy-start.5 = (bf16[512]{0:T(512)(128)(2,1)S(1)}, bf16[512]{0:T(512)(128)(2,1)}, u32[]{:S(2)}) copy-start(bf16[512]{0:T(512)(128)(2,1)} %param.15) | copy-start | bytes 3076
  82.4 69.1 %slice-start.1 = ((bf16[512,512]{1,0:T(8,128)(2,1)}), bf16[504,512]{1,0:T(8,128)(2,1)S(1)}, s32[]{:S(2)}) async-start(bf16[512,512]{1,0:T(8,128)(2,1)} %copy-done), calls=%async_computation.2 | async-start | bytes 1032192 | tf_op jit(solution)/shard_map/slice | solution.py:96
  152.6 6.0 %copy-start.1 = (bf16[512,512]{1,0:T(8,128)(2,1)S(1)}, bf16[512,512]{1,0:T(8,128)(2,1)}, u32[]{:S(2)}) copy-start(bf16[512,512]{1,0:T(8,128)(2,1)} %get-tuple-element.11) | copy-start | bytes 1572868
  162.8 1.0 copy-start.2
Sparse Core Ops, SparseCore 0:
  15.3 135.2 all-gather.4
where the time goes:
time: 227 us; the launch traced here: 226 us
  blocking collectives  167 us (74%)
  local copies, waits for them, and re-layouts  23.7 us (10%)
  between operations  16 us (7%)
  other arithmetic  12.3 us (5%)
  waiting for transfers between devices  4.95 us (2%)
    all_gather x1, blocking collectives, body(): lax.all_gather(raw_tail, 'seq', axis=0, tiled=True)  59.5 us
    all_gather x1, blocking collectives, body(): filter_rows = lax.all_gather(mr_filter, 'seq', axis=0, tiled=True)  56.7 us
    psum x1, blocking collectives, body(): squares_total = lax.psum(jnp.sum(summed * summed, axis=1), 'mp')  51 us
    unnamed x22, local copies, waits for them, and re-layouts  5.46 us
    convert_element_type x1, other arithmetic, body(): mixed_in = (key_feat * value_feat).astype(jnp.bfloat16)  5.34 us
    concatenate x4, local copies, waits for them, and re-layouts, long_conv(): jnp.concatenate([pieces[:-1], pieces[1:]], axis=1)  5.16 us
    all_gather x1, waiting for transfers between devices, body(): lax.all_gather(state_tail, 'seq', axis=0, tiled=True)  4.93 us
    another operation x2, local copies, waits for them, and re-layouts, toeplitz_blocks(): tiled = jnp.tile(pattern, (1, tap_count))[:, :2 * tap_count * tap_count]  4.73 us
  transfers between devices with their start and end apart: 1, of which 1 were waited for; matrix products, arithmetic and copies ran while one was open for 5% of the time, Pallas kernels for 0%

commit v1 on v0

--- a/solution.py
+++ b/solution.py
@@ -57,6 +57,12 @@
     predecessor,
     stretch_lengths,
 ):
+
+    def refer_point(work_x):
+        local_next = lax.all_gather(work_x, axis_name="mp")
+        low = jnp.sum(local_next, axis=0)
+        return low
+
     row_count, width = queries.shape
     device = lax.axis_index("seq")
     filter_rows = lax.all_gather(mr_filter, "seq", axis=0, tiled=True)
@@ -99,7 +105,7 @@
     valid = (jnp.arange(row_count, dtype=jnp.int32) < stretch_lengths[device])[:, None]
     mixed = jnp.where(valid, query_feat * filtered, 0.0).astype(jnp.bfloat16)
     summed = residual.astype(jnp.float32) + mixed.astype(jnp.float32)
-    squares_total = lax.psum(jnp.sum(summed * summed, axis=1), "mp")
+    squares_total = refer_point(jnp.sum(summed * summed, axis=1))
     scale_rows = lax.rsqrt(squares_total / (width * lax.axis_size("mp")) + EPSILON)
     normed = jnp.where(
         valid, summed * scale_rows[:, None] * norm_gain.astype(jnp.float32), 0.0

time: 227 us -> 218 us (0.960)
  blocking collectives: 167 us -> 159 us
    psum x1 -> x0, blocking collectives: 51 us -> none  [body(): squares_total = lax.psum(jnp.sum(summed * summed, axis=1), 'mp')]
    all_gather x0 -> x1, blocking collectives: none -> 42.5 us  [refer_point(): local_next = lax.all_gather(work_x, axis_name='mp')]
where the time goes in v1:
time: 218 us
  blocking collectives  159 us (73%)
  local copies, waits for them, and re-layouts  23.7 us (11%)
  between operations  16 us (7%)
  other arithmetic  12.3 us (6%)
  waiting for transfers between devices  4.95 us (2%)
    all_gather x1, blocking collectives, body(): lax.all_gather(raw_tail, 'seq', axis=0, tiled=True)  59.5 us
    all_gather x1, blocking collectives, body(): filter_rows = lax.all_gather(mr_filter, 'seq', axis=0, tiled=True)  56.7 us
    all_gather x1, blocking collectives, refer_point(): local_next = lax.all_gather(work_x, axis_name='mp')  42.5 us
    unnamed x22, local copies, waits for them, and re-layouts  5.46 us
    convert_element_type x1, other arithmetic, body(): mixed_in = (key_feat * value_feat).astype(jnp.bfloat16)  5.34 us
    concatenate x4, local copies, waits for them, and re-layouts, long_conv(): jnp.concatenate([pieces[:-1], pieces[1:]], axis=1)  5.16 us
    all_gather x1, waiting for transfers between devices, body(): lax.all_gather(state_tail, 'seq', axis=0, tiled=True)  4.93 us
    another operation x2, local copies, waits for them, and re-layouts, toeplitz_blocks(): tiled = jnp.tile(pattern, (1, tap_count))[:, :2 * tap_count * tap_count]  4.73 us
  transfers between devices with their start and end apart: 1, of which 1 were waited for; matrix products, arithmetic and copies ran while one was open for 5% of the time, Pallas kernels for 0%

profile of v1, /device:TPU:1, one launch (start us, length us, event | category | flops | bytes accessed | tf_op | source)
XLA Modules:
  0.0 217.6 jit_solution(11321914940495258178)
XLA Ops:
  7.2 1.0 slice_convert_fusion.20
  8.2 0.8 slice_convert_fusion.1
  9.0 5.3 %multiply_convert_fusion = bf16[512,512]{1,0:T(8,128)(2,1)S(1)} fusion(bf16[512,512]{1,0:T(8,128)(2,1)} %param.11, bf16[512,512]{1,0:T(8,128)(2,1)} %param.10, f32[512]{0:T(512)S(1)} %bitcast.93, f32[512]{0:T(512)S(1)} %bitcast.91, f32[512]{0:T(512)S(1)} %bitcast.67, f32[512]{0:T(512)S(1)} %bitcast.69, f32[512]{0:T(512)S(1)} %bitcast.71, ...), kind=kLoop, calls=%fused_computation.17 | loop fusion | flops 11010048 | bytes 1601536 | tf_op jit(solution)/shard_map/convert_element_type | solution.py:74
  14.4 0.7 slice.328
  16.9 1.0 copy.66
  18.5 56.7 %all-gather.3 = bf16[32,4,32]{2,1,0:T(4,128)(2,1)S(1)} all-gather(bf16[1,4,32]{2,1,0:T(4,128)(2,1)S(1)} %bitcast.104), channel_id=1, replica_groups=mesh['seq'=32,'mp'=16] {'seq'}, dimensions={0}, use_global_device_ids=true | all-gather | bytes 8448 | tf_op jit(solution)/shard_map/all_gather | solution.py:68
  75.8 4.4 %tile.10 = bf16[32,32896]{1,0:T(8,128)(2,1)} reshape(bf16[32,128,257]{2,1,0:T(8,128)(2,1)S(1)} %tile.4) | data formatting | bytes 4210688 | tf_op jit(solution)/shard_map/tile | solution.py:31
  80.3 1.6 slice-done
  82.4 0.8 fusion.27
  83.2 59.5 %all-gather = bf16[256,1536]{1,0:T(8,128)(2,1)S(1)} all-gather(bf16[8,1536]{1,0:T(8,128)(2,1)S(1)} %pad_maximum_fusion.4), channel_id=2, replica_groups=mesh['seq'=32,'mp'=16] {'seq'}, dimensions={0}, use_global_device_ids=true | all-gather | bytes 811008 | tf_op jit(solution)/shard_map/all_gather | solution.py:83
  143.6 1.3 copy.75
  145.7 4.9 %all-gather.7.cloned.1.call-done = bf16[4096,512]{1,0:T(8,128)(2,1)} async-done(((bf16[128,512]{1,0:T(8,128)(2,1)}), bf16[4096,512]{1,0:T(8,128)(2,1)}) %all-gather.7.cloned.1.call-update) | async-done | bytes 4194320 | tf_op jit(solution)/shard_map/all_gather | solution.py:82
  150.6 0.9 select_bitcast_fusion
  151.5 1.0 pad_maximum_fusion
  152.6 2.1 copy.69
  154.7 2.0 concatenate.42
  156.7 1.9 copy.71
  158.6 1.0 copy.70
  159.6 1.2 concatenate.44
  160.9 1.9 fusion.2
  163.8 2.1 multiply_reduce_fusion
  165.9 42.5 %all-gather.4 = f32[16,1,512]{2,1,0:T(1,128)S(1)} all-gather(f32[1,1,512]{2,1,0:T(1,128)S(1)} %bitcast.102), channel_id=4, replica_groups=mesh['seq'=32,'mp'=16] {'mp'}, dimensions={0}, use_global_device_ids=true | all-gather | bytes 34816 | tf_op jit(solution)/shard_map/all_gather | solution.py:62
  208.5 1.0 copy.76
  209.7 1.0 copy.77
  (45 shorter events, 4.8 us)
Async XLA Ops:
  7.2 8.0 %copy-start.6 = (s32[32]{0:T(128)S(1)}, s32[32]{0:T(128)}, u32[]{:S(2)}) copy-start(s32[32]{0:T(128)} %param.16) | copy-start | bytes 388
  7.2 9.7 %copy-start.3 = (bf16[512,512]{1,0:T(8,128)(2,1)S(1)}, bf16[512,512]{1,0:T(8,128)(2,1)}, u32[]{:S(2)}) copy-start(bf16[512,512]{1,0:T(8,128)(2,1)} %param.9) | copy-start | bytes 1572868
  7.2 143.4 %all-gather.7.cloned.1.call-start = ((), (), s32[]{:S(2)}) async-start(), calls=%async_computation | async-start | bytes 4325376 | tf_op jit(solution)/shard_map/all_gather | solution.py:82
  8.2 10.2 %copy-start.4 = (bf16[4,32]{1,0:T(4,128)(2,1)S(1)}, bf16[4,32]{1,0:T(4,128)(2,1)}, u32[]{:S(2)}) copy-start(bf16[4,32]{1,0:T(4,128)(2,1)} %param.14) | copy-start | bytes 772
  14.4 61.1 %copy-start = (bf16[512,512]{1,0:T(8,128)(2,1)}, bf16[512,512]{1,0:T(8,128)(2,1)S(1)}, u32[]{:S(2)}) copy-start(bf16[512,512]{1,0:T(8,128)(2,1)S(1)} %multiply_convert_fusion) | copy-start | bytes 1572868
  80.3 1.6 slice-start
  81.9 1.3 slice-start.2
  81.9 61.1 %copy-start.7 = (s32[32]{0:T(128)S(1)}, s32[32]{0:T(128)}, u32[]{:S(2)}) copy-start(s32[32]{0:T(128)} %param.17) | copy-start | bytes 388
  82.4 62.5 %copy-start.5 = (bf16[512]{0:T(512)(128)(2,1)S(1)}, bf16[512]{0:T(512)(128)(2,1)}, u32[]{:S(2)}) copy-start(bf16[512]{0:T(512)(128)(2,1)} %param.15) | copy-start | bytes 3076
  82.4 69.1 %slice-start.1 = ((bf16[512,512]{1,0:T(8,128)(2,1)}), bf16[504,512]{1,0:T(8,128)(2,1)S(1)}, s32[]{:S(2)}) async-start(bf16[512,512]{1,0:T(8,128)(2,1)} %copy-done), calls=%async_computation.2 | async-start | bytes 1032192 | tf_op jit(solution)/shard_map/slice | solution.py:102
  152.6 6.0 %copy-start.1 = (bf16[512,512]{1,0:T(8,128)(2,1)S(1)}, bf16[512,512]{1,0:T(8,128)(2,1)}, u32[]{:S(2)}) copy-start(bf16[512,512]{1,0:T(8,128)(2,1)} %get-tuple-element.11) | copy-start | bytes 1572868
  162.8 1.0 copy-start.2
Sparse Core Ops, SparseCore 0:
  15.3 135.2 all-gather.6
